TPU v7x, 512 devices: a whole 4x4x16 slice. The times are simulated.
512 devices in a mesh: group: 16 (over x, y), member: 32 (over z, core).
Axes of the slice: x: 4, y: 4, z: 16, core: 2. Of those that a mesh axis runs over, the one named last changes fastest.
Arguments:
- features: float32 [65536, 128], P(('group', 'member')), may hold values from -6 to 6
- w_self: float32 [128, 256], replicated, may hold values from -0.5 to 0.5
- w_neigh: float32 [128, 256], replicated, may hold values from -0.5 to 0.5
- bias: float32 [256], replicated, may hold values from -3 to 3
- cotangent: float32 [65536, 256], P(('group', 'member')), may hold values from -6 to 6
- edge_src: int32 [512, 1024], P(('group', 'member')), may hold values from 0 to 4607, as said below
- edge_dst: int32 [512, 1024], P(('group', 'member')), may hold values from 0 to 4095
- edge_count: int32 [512], P(('group', 'member')), may hold values from 768 to 1024, as said below
Outputs:
- hidden: float32 [65536, 256], P(('group', 'member'))
- feature_grad: float32 [65536, 128], P(('group', 'member'))
- grad_self: float32 [128, 256], replicated
- grad_neigh: float32 [128, 256], replicated
- grad_bias: float32 [256], replicated
Inputs may be any that keep to these rules, and one draw needn't show every extreme that they name: `edge_src`: sources are drawn at random; about a quarter of the used slots name hubs. `edge_count`: some device uses all 1024 slots.
All inputs are finite; a program needn't handle non-finite values.
Results may differ from a plain program's by a relative error of at most 0.000073.
Values sent between devices are 32-bit elements; how exact they have to be, the bound alone decides.
A program may use at most 64 MiB of HBM per device.

v0:
```python
import jax
import jax.numpy as jnp
from jax import lax
from jax.sharding import PartitionSpec as P

HUB_DEV = 1


def on_device(features, w_self, w_neigh, bias, cotangent, edge_src, edge_dst, edge_count):
    highest = lax.Precision.HIGHEST
    rows_dev = features.shape[0]
    members = lax.axis_size("member")
    groups = lax.axis_size("group")
    group_rows = rows_dev * members
    slots = edge_src.shape[1]
    member_number = lax.axis_index("member")
    first_own = member_number * rows_dev

    def fetch_rows(values_in, lookup):
        gathered = lax.all_gather(values_in, "member", axis=0, tiled=True)
        inside = lookup < group_rows
        picked = jnp.take(gathered, jnp.clip(lookup, 0, group_rows - 1), axis=0)
        return jnp.where(inside[:, None], picked, 0.0)

    source = edge_src[0]
    target = edge_dst[0]
    in_use = (lax.iota(jnp.int32, slots) < edge_count[0]).astype(jnp.float32)
    hub_table = lax.all_gather(features[:HUB_DEV], ("group", "member"), axis=0, tiled=True)
    hub_count = hub_table.shape[0]
    from_hub = source >= group_rows
    hub_picked = jnp.take(hub_table, jnp.clip(source - group_rows, 0, hub_count - 1), axis=0)
    local_picked = fetch_rows(features, source)
    neighbour = jnp.where(from_hub[:, None], hub_picked, local_picked) * in_use[:, None]
    partial_value = jax.ops.segment_sum(neighbour, target, num_segments=group_rows)
    partial_count = jax.ops.segment_sum(in_use, target, num_segments=group_rows)
    summed = lax.psum_scatter(partial_value, "member", scatter_dimension=0, tiled=True)
    group_degree = lax.psum(partial_count, "member")
    degree = lax.dynamic_slice_in_dim(group_degree, first_own, rows_dev, 0)
    divisor = jnp.maximum(degree, 1.0)
    neigh_mean = summed / divisor[:, None]
    pre_act = (
        jnp.dot(features, w_self, precision=highest)
        + jnp.dot(neigh_mean, w_neigh, precision=highest)
        + bias
    )
    sigmoid_z = jax.nn.sigmoid(pre_act)
    hidden = pre_act * sigmoid_z
    pre_grad = cotangent * sigmoid_z * (1.0 + pre_act * (1.0 - sigmoid_z))
    mean_grad = jnp.dot(pre_grad, w_neigh.T, precision=highest) / divisor[:, None]
    edge_values = fetch_rows(mean_grad, target) * in_use[:, None]
    source_part = jax.ops.segment_sum(edge_values, source, num_segments=group_rows + hub_count)
    group_grad = lax.psum_scatter(
        source_part[:group_rows], "member", scatter_dimension=0, tiled=True
    )
    hub_part = source_part[group_rows:]
    self_part = jnp.dot(features.T, pre_grad, precision=highest)
    neigh_part = jnp.dot(neigh_mean.T, pre_grad, precision=highest)
    bias_part = jnp.sum(pre_grad, axis=0)
    self_total, neigh_total, bias_total, hub_total = lax.psum(
        (self_part, neigh_part, bias_part, hub_part), ("group", "member")
    )
    device_number = lax.axis_index(("group", "member"))
    own_hubs = lax.dynamic_slice_in_dim(hub_total, device_number * HUB_DEV, HUB_DEV, 0)
    feature_grad = jnp.dot(pre_grad, w_self.T, precision=highest) + group_grad
    feature_grad = feature_grad.at[:HUB_DEV].add(own_hubs)
    scale = 1.0 / jnp.sqrt(jnp.float32(rows_dev * members * groups))
    return (hidden, feature_grad, self_total * scale, neigh_total * scale, bias_total * scale)


def solution(mesh):
    return jax.shard_map(
        on_device,
        mesh=mesh,
        in_specs=(
            P(("group", "member"), None),
            P(),
            P(),
            P(),
            P(("group", "member"), None),
            P(("group", "member"), None),
            P(("group", "member"), None),
            P(("group", "member")),
        ),
        out_specs=(P(("group", "member"), None), P(("group", "member"), None), P(), P(), P()),
        check_vma=False,
    )
```

profile of v0, /device:TPU:1, one launch (start us, length us, event | category | flops | bytes accessed | tf_op | source)
XLA Modules:
  0.0 912.2 jit_solution(5625465885781866832)
XLA Ops:
  7.2 0.7 all-gather.4.cloned.1.call-update
  8.6 0.7 compare_reduce_fusion.2
  9.3 0.7 slice_bitcast_fusion
  10.0 113.0 %all-gather = f32[512,1,128]{2,1,0:T(1,128)S(1)} all-gather(f32[1,1,128]{2,1,0:T(1,128)S(1)} %slice_bitcast_fusion), channel_id=1, replica_groups=mesh['group'=16,'member'=32] {'group','member'}, dimensions={0}, use_global_device_ids=true | all-gather | bytes 262656 | tf_op jit(solution)/shard_map/all_gather | solution.py:28
  123.0 0.7 add_clamp_fusion
  123.7 0.7 compare_select_fusion
  124.5 23.3 %scatter_custom_fusion = f32[4096,128]{1,0:T(8,128)} fusion(s32[1024]{0:T(1024)} %bitcast.32, f32[]{:T(128)} %constant.72.clone.1, f32[1024]{0:T(1024)S(1)} %get-tuple-element.43, f32[]{:T(128)} %constant.78.clone.1, pred[1024]{0:T(1024)(128)(4,1)S(1)} %get-tuple-element.44, pred[1024]{0:T(1024)(128)(4,1)S(1)} %get-tuple-element.34, ...), kind=kCustom, calls=%fused_computation.13 | custom fusion | flops 786432 | bytes 4474368 | tf_op jit(solution)/shard_map/scatter-add | solution.py:34
  147.9 0.6 copy-done.4
  148.5 5.9 scatter_custom_fusion.1
  154.4 88.9 %psum.35 = f32[4096]{0:T(1024)S(1)} all-reduce(f32[4096]{0:T(1024)S(1)} %scatter_custom_fusion.1), channel_id=1, replica_groups=mesh['group'=16,'member'=32] {'member'}, use_global_device_ids=true, to_apply=%region_3.5 | all-reduce | flops 4096 | bytes 32768 | tf_op jit(solution)/shard_map/psum | solution.py:37
  243.4 0.3 fusion.34
  243.7 6.6 reduce-scatter.3.cloned.1.call-done
  250.2 1.9 fusion.33
  252.1 0.9 convolution_divide_fusion
  253.0 0.2 all-reduce.3.cloned.1.call-start
  253.3 1.0 convolution_bitcast_fusion
  254.4 1.9 fusion.24
  256.3 69.5 %all-gather.6.cloned.1.call-done = f32[4096,128]{1,0:T(8,128)} async-done(((f32[128,128]{1,0:T(8,128)}), f32[4096,128]{1,0:T(8,128)}) %all-gather.6.cloned.1.call-update) | async-done | bytes 2097168 | tf_op jit(solution)/shard_map/all_gather | solution.py:20
  325.8 12.8 %scatter_custom_fusion.2 = f32[4608,128]{1,0:T(8,128)S(1)} fusion(s32[1024]{0:T(1024)} %bitcast.26, f32[]{:T(128)} %constant.72.clone.1, f32[1024]{0:T(1024)S(1)} %get-tuple-element.43, f32[]{:T(128)} %constant.78.clone.1, pred[1024]{0:T(1024)(128)(4,1)S(1)} %compare_and_fusion, pred[1024]{0:T(1024)(128)(4,1)S(1)} %compare_reduce_fusion, ...), kind=kCustom, calls=%fused_computation.6 | custom fusion | flops 524288 | bytes 4468224 | tf_op jit(solution)/shard_map/scatter-add | solution.py:51
  338.6 0.7 slice.40
  339.4 1.5 slice.38
  340.9 103.4 %psum.39 = f32[256]{0:T(256)S(1)} all-reduce(f32[256]{0:T(256)S(1)} %get-tuple-element.38), channel_id=1, replica_groups=mesh['group'=16,'member'=32] {'group','member'}, use_global_device_ids=true, to_apply=%region_10.12 | all-reduce | flops 256 | bytes 2048 | tf_op jit(solution)/shard_map/psum | solution.py:59
  444.3 0.6 broadcast_multiply_fusion.2
  444.9 351.6 %all-reduce.3.cloned.1.call-done = (f32[512,128]{1,0:T(8,128)}, f32[128,256]{0,1:T(8,128)}, f32[128,256]{0,1:T(8,128)}) async-done(((f32[512,128]{1,0:T(8,128)}, f32[128,256]{0,1:T(8,128)}, f32[128,256]{0,1:T(8,128)}), (f32[512,128]{1,0:T(8,128)}, f32[128,256]{0,1:T(8,128)}, f32[128,256]{0,1:T(8,128)})) %all-reduce.3.cloned.1.call-update) | async-done | bytes 524304 | tf_op jit(solution)/shard_map/psum | solution.py:59
  796.5 0.9 broadcast_multiply_fusion.1
  797.4 0.8 copy.22
  798.1 0.9 broadcast_multiply_fusion
  799.1 0.8 copy.23
  799.8 103.4 %reduce-scatter.5.cloned.1.call-done = f32[128,128]{1,0:T(8,128)} async-done(((f32[4096,128]{1,0:T(8,128)}), f32[128,128]{1,0:T(8,128)}) %reduce-scatter.5.cloned.1.call-update) | async-done | bytes 65552 | tf_op jit(solution)/shard_map/reduce_scatter | solution.py:52
  903.2 1.1 convolution_add_fusion.1
  904.3 0.7 slice_add_fusion
  905.1 0.6 copy-done.3
  (30 shorter events, 0.4 us)
Async XLA Ops:
  7.2 243.1 %copy-start = (f32[128,256]{1,0:T(8,128)S(1)}, f32[128,256]{1,0:T(8,128)}, u32[]{:S(2)}) copy-start(f32[128,256]{1,0:T(8,128)} %param.14) | copy-start | bytes 393220
  7.2 117.3 %all-gather.4.cloned.1.call-start = ((), (), s32[]{:S(2)}) async-start(), calls=%async_computation.2 | async-start | bytes 2162688 | tf_op jit(solution)/shard_map/all_gather | solution.py:20
  7.9 242.3 %reduce-scatter.3.cloned.1.call-start = ((), (), s32[]{:S(2)}) async-start(), calls=%async_computation.3 | async-start | bytes 2162688 | tf_op jit(solution)/shard_map/reduce_scatter | solution.py:36
  147.8 0.7 copy-start.4
  147.8 95.6 %copy-start.1 = (f32[128,128]{1,0:T(8,128)S(1)}, f32[128,128]{1,0:T(8,128)}, u32[]{:S(2)}) copy-start(f32[128,128]{1,0:T(8,128)} %param.12) | copy-start | bytes 196612
  147.8 95.6 %copy-start.2 = (f32[128,256]{1,0:T(8,128)S(1)}, f32[128,256]{1,0:T(8,128)}, u32[]{:S(2)}) copy-start(f32[128,256]{1,0:T(8,128)} %param.13) | copy-start | bytes 393220
  147.8 102.4 %copy-start.5 = (f32[128,256]{1,0:T(8,128)S(1)}, f32[128,256]{1,0:T(8,128)}, u32[]{:S(2)}) copy-start(f32[128,256]{1,0:T(8,128)} %param.16) | copy-start | bytes 393220
  147.8 102.4 %copy-start.6 = (f32[256]{0:T(256)S(1)}, f32[256]{0:T(256)}, u32[]{:S(2)}) copy-start(f32[256]{0:T(256)} %param.15) | copy-start | bytes 3076
  147.8 178.0 %all-gather.6.cloned.1.call-start = ((), (), s32[]{:S(2)}) async-start(), calls=%async_computation.4 | async-start | bytes 2162688 | tf_op jit(solution)/shard_map/all_gather | solution.py:20
  253.0 543.4 %all-reduce.3.cloned.1.call-start = ((), (), s32[]{:S(2)}) async-start(), calls=%async_computation.6 | async-start | bytes 1048576 | tf_op jit(solution)/shard_map/psum | solution.py:59
  339.3 563.9 %reduce-scatter.5.cloned.1.call-start = ((), (), s32[]{:S(2)}) async-start(), calls=%async_computation.5 | async-start | bytes 2162688 | tf_op jit(solution)/shard_map/reduce_scatter | solution.py:52
  905.1 0.6 copy-start.3
Sparse Core Ops, SparseCore 0:
  10.1 77.4 all-gather.3
  147.9 102.2 reduce-scatter.2
  253.1 72.6 all-gather.5
  339.4 456.9 all-reduce.2
  799.1 104.0 reduce-scatter.4
where the time goes:
time: 915 us; the launch traced here: 912 us
  waiting for transfers between devices  532 us (58%)
  blocking collectives  305 us (33%)
  other arithmetic  47.3 us (5%)
  between operations  14.6 us (2%)
    psum x1, waiting for transfers between devices, on_device(): lax.psum((self_part, neigh_part, bias_part, hub_part), ('group', 'member'))  352 us
    all_gather x1, blocking collectives, on_device(): lax.all_gather(features[:HUB_DEV], ('group', 'member'), axis=0, tiled=True)  113 us
    psum x1, blocking collectives, on_device(): lax.psum((self_part, neigh_part, bias_part, hub_part), ('group', 'member'))  103 us
    reduce_scatter x1, waiting for transfers between devices, on_device(): lax.psum_scatter(source_part[:group_rows], 'member', scatter_dimension=0,...  103 us
    psum x1, blocking collectives, on_device(): group_degree = lax.psum(partial_count, 'member')  88.9 us
    all_gather x2, waiting for transfers between devices, fetch_rows(): gathered = lax.all_gather(values_in, 'member', axis=0, tiled=True)  69.5 us
    scatter-add x1, other arithmetic, on_device(): jax.ops.segment_sum(neighbour, target, num_segments=group_rows)  23.3 us
  transfers between devices with their start and end apart: 5, of which 4 were waited for; matrix products, arithmetic and copies ran while one was open for 2% of the time, Pallas kernels for 0%

commit v1 on v0

v1 whole, which is shorter than its diff:
```python
import functools

import jax
import jax.numpy as jnp
from jax import lax
from jax.experimental import pallas as pl
from jax.experimental.pallas import tpu as pltpu
from jax.sharding import PartitionSpec as P

f32, bf16, i32 = jnp.float32, jnp.bfloat16, jnp.int32
MESH = pl.DeviceIdType.MESH
G, M = 16, 32
ROWS = 128
IN, HID = 128, 256
CHUNK = 1024
LOCAL = M * ROWS
LO = 256
HI_V = LOCAL // LO
HI_S = HI_V + G * M // LO
NT = (((1,), (1,)), ((), ()))


def dot(a, b, dims=(((1,), (0,)), ((), ()))):
    return lax.dot_general(a, b, dims, precision=lax.Precision.HIGHEST, preferred_element_type=f32)


def split8(x):
    high = x.astype(bf16).astype(f32)
    return jnp.concatenate([high, x - high], axis=0)


def fold8(x):
    return x + pltpu.roll(x, 4, 0)


def alternate(k, n):
    odd = lax.rem(k, 2)
    return odd * ((k + 1) // 2) + (1 - odd) * (n - k // 2)


def kernel(
    feat, w_self, w_neigh, bias, cot, e_src, e_dst, e_cnt,
    hid_o, fg_o, gs_o, gn_o, gb_o,
    oh_s, oh_d, r0, r1, v0, v1, acc, tab,
    hubrx, erx, fts, frx, hts, hrx, sums, sumrx, mgs, mgrx,
    g1s, g1rx, p2s, p2rx, p3s, p3rx, p4s, p4rx,
    bs, brx, hbs, hbrx, h2s, h2rx,
    ssem, rsem, esem,
):
    g, m = lax.axis_index("group"), lax.axis_index("member")
    core, z = lax.rem(m, 2), m // 2
    sib = m + 1 - 2 * core
    sub16 = lax.broadcasted_iota(i32, (16, 128), 0)
    iota16 = sub16.astype(f32).astype(bf16)
    pat16 = (sub16 // 8).astype(f32).astype(bf16)
    one16 = jnp.ones((16, 128), bf16)
    zero16 = jnp.zeros((16, 128), bf16)

    def copy_to(src, dst, k, gg, mm, recv=None):
        return pltpu.make_async_remote_copy(
            src_ref=src, dst_ref=dst, send_sem=ssem.at[k],
            recv_sem=rsem.at[k] if recv is None else recv,
            device_id=(gg, mm), device_id_type=MESH,
        )

    def over_members(src, dst, k, own=True):
        @pl.loop(1, M)
        def _(step):
            to = lax.rem(m + alternate(step, M), M)
            copy_to(src.at[to], dst.at[m], k, g, to).start()
        if own:
            dst[m] = src[m]

    def over_groups(src, dst, k):
        @pl.loop(1, G)
        def _(step):
            to = lax.rem(g + step, G)
            copy_to(src.at[to], dst.at[g], k, to, m).start()
        dst[g] = src[g]

    def wait(buf, n, sem):
        view = buf.at[pl.ds(0, n)]
        pltpu.make_async_copy(view, view, sem).wait()

    barrier = pltpu.get_barrier_semaphore()

    @pl.loop(1, M)
    def _(step):
        pl.semaphore_signal(barrier, inc=1, device_id=(g, lax.rem(m + step, M)), device_id_type=MESH)

    @pl.loop(1, G)
    def _(step):
        pl.semaphore_signal(barrier, inc=1, device_id=(lax.rem(g + step, G), m), device_id_type=MESH)

    def rows4(dst, x):
        for i in range(M):
            dst[i] = x[4 * i : 4 * i + 4, :]

    def joined(src):
        return jnp.concatenate([src[i] for i in range(M)], axis=0)

    with jax.named_scope("pack"):
        ft = feat[...].T
        rows4(fts, ft)
        src = e_src[...]
        hub = src - LOCAL
        src = jnp.where(hub >= 0, LOCAL + ((hub & (M - 1)) * G + (hub >> 5)), src)
        used = lax.broadcasted_iota(i32, (1, CHUNK), 1) < e_cnt[0]
        dst = jnp.where(used, e_dst[...], LOCAL)
        for r in range(8):
            erx[m, r : r + 1, :] = src[:, 128 * r : 128 * r + 128]
            erx[m, 8 + r : 9 + r, :] = dst[:, 128 * r : 128 * r + 128]

    pl.semaphore_wait(barrier, M - 1 + G - 1)

    hub_tile = feat.at[pl.ds(0, 8)]

    @pl.loop(1, G)
    def _(step):
        copy_to(hub_tile, hubrx.at[g], 0, lax.rem(g + step, G), m).start()

    hubrx[g] = feat[0:8, :]
    copy_to(erx.at[m], erx.at[m], 1, g, sib, esem.at[m]).start()

    @pl.loop(1, M // 2)
    def _(step):
        to = lax.rem(z + alternate(step, M // 2), M // 2) * 2 + core
        copy_to(erx.at[m], erx.at[m], 1, g, to, esem.at[m]).start()

    over_members(fts, frx, 2)

    wait(hubrx, G - 1, rsem.at[0])
    hub_rows = jnp.concatenate([hubrx[i][0:1, :] for i in range(G)] + [jnp.zeros((128 - G, 128), f32)], axis=0)
    rows4(hts, hub_rows.T)
    over_members(hts, hrx, 3)

    def one_hot(low, ref, slot):
        for r in range(8):
            row = jnp.broadcast_to(low[r : r + 1, :].astype(f32), (16, 128)).astype(bf16) - iota16
            for t in range(LO // 16):
                ref[slot, 16 * t : 16 * t + 16, 128 * r : 128 * r + 128] = jnp.where(
                    row == jnp.array(16 * t, bf16), one16, zero16
                )

    def both_hots(slot):
        one_hot(erx[slot, 0:8, :] & (LO - 1), oh_s, slot)
        one_hot(erx[slot, 8:16, :] & (LO - 1), oh_d, slot)

    def edge_wait(slot):
        pltpu.make_async_copy(erx.at[slot], erx.at[slot], esem.at[slot]).wait()

    both_hots(m)

    @pl.loop(1, M // 2)
    def _(step):
        slot = lax.rem(z + M // 2 - alternate(step, M // 2), M // 2) * 2 + core
        edge_wait(slot)
        copy_to(erx.at[slot], erx.at[slot], 1, g, sib, esem.at[slot]).start()
        both_hots(slot)

    edge_wait(sib)
    both_hots(sib)

    @pl.loop(1, M // 2)
    def _(step):
        slot = lax.rem(z + M // 2 - alternate(step, M // 2), M // 2) * 2 + 1 - core
        edge_wait(slot)
        both_hots(slot)

    def table(src):
        for t in range(HI_V // 2):
            for c in range(2):
                tab[16 * t : 16 * t + 16, 128 * c : 128 * c + 128] = jnp.concatenate(
                    [split8(src[4 * t + c]), split8(src[4 * t + 2 + c])], axis=0
                ).astype(bf16)

    def spread(values, high, v, n):
        w16 = jnp.concatenate([values, values], axis=0).astype(bf16)
        row = jnp.broadcast_to(high.astype(f32), (16, 128)).astype(bf16) - pat16
        for t in range(n // 2):
            v[16 * t : 16 * t + 16, :] = jnp.where(row == jnp.array(2 * t, bf16), w16, zero16)

    def aggregate(rows_in, n_in, n_out, forward, between):
        oh_in, oh_out = (oh_s, oh_d) if forward else (oh_d, oh_s)

        def gather(j, r):
            r[0:rows_in, :] = jnp.dot(tab[0:rows_in, :], oh_in[j], preferred_element_type=f32)

        def place(j, r, v):
            s_hi, d_hi = erx[j, 0:8, :] >> 8, erx[j, 8:16, :] >> 8
            in_hi, out_hi = (s_hi, d_hi) if forward else (d_hi, s_hi)
            for q in range(8):
                cols = pl.ds(128 * q, 128)
                high = jnp.broadcast_to(in_hi[q : q + 1, :], (8, 128))
                w = jnp.zeros((8, 128), f32)
                for h in range(n_in):
                    w = jnp.where(high == h, r[8 * h : 8 * h + 8, cols], w)
                spread(w, out_hi[q : q + 1, :], v.at[:, cols], n_out)
                if forward:
                    mine = jnp.broadcast_to(out_hi[q : q + 1, :], (16, 128)) == z
                    v[8 * n_out : 8 * n_out + 16, cols] = jnp.where(
                        mine & (sub16 == 0), jnp.float32(1), jnp.float32(0)
                    ).astype(bf16)

        def add(j, v):
            acc[...] += lax.dot_general(v[...], oh_out[j], NT, preferred_element_type=f32)

        acc[...] = jnp.zeros_like(acc)
        v1[...] = jnp.zeros_like(v1)
        gather(0, r0)

        def pair(i):
            j = 2 * i
            add(jnp.maximum(j - 1, 0), v1)
            place(j, r0, v0)
            gather(j + 1, r1)
            add(j, v0)
            place(j + 1, r1, v1)
            gather(jnp.minimum(j + 2, M - 1), r0)

        parts = len(between) + 1
        for part in range(parts):
            pl.loop(part * M // 2 // parts, (part + 1) * M // 2 // parts)(pair)
            if part < parts - 1:
                between[part]()
        add(M - 1, v1)

    def unpack(dst):
        for h in range(HI_V):
            for c in range(2):
                dst[2 * h + c] = fold8(acc[8 * h : 8 * h + 8, 128 * c : 128 * c + 128])[0:4, :]

    wait(frx, M - 1, rsem.at[2])
    with jax.named_scope("table"):
        table(frx)
    wait(hrx, M - 1, rsem.at[3])
    with jax.named_scope("hub_table"):
        for c in range(2):
            hubs = jnp.zeros((8, 128), f32)
            for k in range(8):
                both = jnp.concatenate([hrx[8 * c + k], hrx[16 + 8 * c + k]], axis=0)
                hubs = hubs + (pltpu.roll(both, 16 * k, 1) if k else both)
            tab[8 * HI_V : 8 * HI_S, 128 * c : 128 * c + 128] = jnp.concatenate(
                [split8(hubs[0:4, :]), split8(hubs[4:8, :])], axis=0
            ).astype(bf16)

    self_act = dot(feat[...], w_self[...]) + bias[...]
    with jax.named_scope("forward"):
        aggregate(8 * HI_S, HI_S, HI_V, True, [])
    with jax.named_scope("sums"):
        unpack(sums)
        over_members(sums, sumrx, 4)
        own = acc[8 * HI_V : 8 * HI_V + 1, :]
        degree = jnp.where(core == 0, own[:, 0:128], own[:, 128:256])
        inverse = 1.0 / jnp.maximum(degree, 1.0)
        wait(sumrx, M - 1, rsem.at[4])
    with jax.named_scope("dense"):
        mean_t = joined(sumrx) * inverse
        pre_act = self_act + dot(mean_t.T, w_neigh[...])
        sig = jax.nn.sigmoid(pre_act)
        hid_o[...] = pre_act * sig
        pre_grad = cot[...] * sig * (1.0 + pre_act * (1.0 - sig))
        rows4(mgs, dot(w_neigh[...], pre_grad, NT) * inverse)
        over_members(mgs, mgrx, 5)
        grad_s = dot(ft, pre_grad)
        grad_n = dot(mean_t, pre_grad)
        grad_b = jnp.broadcast_to(jnp.sum(pre_grad, axis=0, keepdims=True), (8, HID))
        for p in range(G):
            half = grad_s if p < G // 2 else grad_n
            at = 16 * (p % (G // 2))
            g1s[p, 0:16, :] = half[at : at + 16, :]
            g1s[p, 16:24, :] = grad_b
        over_groups(g1s, g1rx, 6)
        fg_o[...] = dot(pre_grad, w_self[...], NT)

    scale = 1.0 / (float(G * M * ROWS) ** 0.5)

    def reduce_groups():
        wait(g1rx, G - 1, rsem.at[6])
        total = g1rx[0]
        for i in range(1, G):
            total = total + g1rx[i]
        b0, b1 = total[16:17, 0:128], total[16:17, 128:256]
        rest = jnp.concatenate([b0, b1, jnp.zeros((1, 128), f32)], axis=0)
        for i in range(M):
            c = 128 * (i % 2)
            p2s[i] = jnp.concatenate([total[i // 2 : i // 2 + 1, c : c + 128], rest], axis=0)
        over_members(p2s, p2rx, 7)

    def reduce_members():
        wait(p2rx, M - 1, rsem.at[7])
        total = p2rx[0]
        for i in range(1, M):
            total = total + p2rx[i]
        total = total * scale
        gb_o[:, 0:128] = total[1:2, :]
        gb_o[:, 128:256] = total[2:3, :]
        p3s[...] = total

        @pl.loop(1, M)
        def _(step):
            to = lax.rem(m + alternate(step, M), M)
            copy_to(p3s, p3rx.at[m], 8, g, to).start()

        p3rx[m] = total

    def collect_members():
        wait(p3rx, M - 1, rsem.at[8])
        for i in range(M):
            c = 128 * (i % 2)
            p4s[i // 2 : i // 2 + 1, c : c + 128] = p3rx[i][0:1, :]

        @pl.loop(1, G)
        def _(step):
            copy_to(p4s, p4rx.at[g], 9, lax.rem(g + step, G), m).start()

        p4rx[g] = p4s[...]

    wait(mgrx, M - 1, rsem.at[5])
    with jax.named_scope("backward"):
        table(mgrx)
        aggregate(8 * HI_V, HI_V, HI_S, False, [reduce_groups, reduce_members, collect_members])
    with jax.named_scope("gradients"):
        for c in range(4):
            hubs = fold8(acc[8 * HI_V + 8 * (c // 2) : 8 * HI_V + 8 * (c // 2) + 8, 128 * (c % 2) : 128 * (c % 2) + 128])
            for k in range(8):
                hbs[8 * c + k] = (pltpu.roll(hubs, 128 - 16 * k, 1) if k else hubs)[0:4, :]
        over_members(hbs, hbrx, 10)
        unpack(bs)
        over_members(bs, brx, 11)
        wait(p4rx, G - 1, rsem.at[9])
        for p in range(G // 2):
            gs_o[16 * p : 16 * p + 16, :] = p4rx[p]
            gn_o[16 * p : 16 * p + 16, :] = p4rx[G // 2 + p]
        wait(hbrx, M - 1, rsem.at[10])
        hub_t = joined(hbrx).T
        for p in range(G):
            h2s[p] = jnp.broadcast_to(hub_t[p : p + 1, :], (8, 128))
        over_groups(h2s, h2rx, 12)
        wait(brx, M - 1, rsem.at[11])
        fg_o[...] += joined(brx).T
        wait(h2rx, G - 1, rsem.at[12])
        total = h2rx[0]
        for i in range(1, G):
            total = total + h2rx[i]
        first = lax.broadcasted_iota(i32, (8, 128), 0) == 0
        fg_o[0:8, :] += jnp.where(first, total, 0.0)

    wait(hubrx, G - 1, ssem.at[0])
    wait(erx, M - 1, ssem.at[1])
    wait(frx, M - 1, ssem.at[2])
    wait(hrx, M - 1, ssem.at[3])
    wait(sumrx, M - 1, ssem.at[4])
    wait(mgrx, M - 1, ssem.at[5])
    wait(g1rx, G - 1, ssem.at[6])
    wait(p2rx, M - 1, ssem.at[7])
    wait(p3rx, M - 1, ssem.at[8])
    wait(p4rx, G - 1, ssem.at[9])
    wait(hbrx, M - 1, ssem.at[10])
    wait(brx, M - 1, ssem.at[11])
    wait(h2rx, G - 1, ssem.at[12])


def on_device(features, w_self, w_neigh, bias, cotangent, edge_src, edge_dst, edge_count):
    vmem = pl.BlockSpec(memory_space=pltpu.VMEM)
    smem = pl.BlockSpec(memory_space=pltpu.SMEM)
    quads = pltpu.VMEM((M, 4, 128), f32)
    tiles = pltpu.VMEM((G, 8, 128), f32)
    scratch = [
        pltpu.VMEM((M, LO, CHUNK), bf16), pltpu.VMEM((M, LO, CHUNK), bf16),
        pltpu.VMEM((8 * HI_S, CHUNK), f32), pltpu.VMEM((8 * HI_S, CHUNK), f32),
        pltpu.VMEM((8 * HI_S, CHUNK), bf16), pltpu.VMEM((8 * HI_S, CHUNK), bf16),
        pltpu.VMEM((8 * HI_S, LO), f32), pltpu.VMEM((8 * HI_S, LO), bf16),
        tiles, pltpu.VMEM((M, 16, 128), i32), quads, quads, quads, quads, quads, quads, quads, quads,
        pltpu.VMEM((G, 24, HID), f32), pltpu.VMEM((G, 24, HID), f32), quads, quads,
        pltpu.VMEM((4, 128), f32), quads, pltpu.VMEM((16, HID), f32), pltpu.VMEM((G, 16, HID), f32),
        quads, quads, quads, quads, tiles, tiles,
        pltpu.SemaphoreType.DMA((13,)), pltpu.SemaphoreType.DMA((13,)), pltpu.SemaphoreType.DMA((M,)),
    ]
    hidden, feature_grad, grad_self, grad_neigh, grad_bias = pl.pallas_call(
        kernel,
        out_shape=(
            jax.ShapeDtypeStruct((ROWS, HID), f32),
            jax.ShapeDtypeStruct((ROWS, IN), f32),
            jax.ShapeDtypeStruct((IN, HID), f32),
            jax.ShapeDtypeStruct((IN, HID), f32),
            jax.ShapeDtypeStruct((1, HID), f32),
        ),
        in_specs=[vmem] * 7 + [smem],
        out_specs=[vmem] * 5,
        scratch_shapes=scratch,
        compiler_params=pltpu.CompilerParams(
            collective_id=0, has_side_effects=True, vmem_limit_bytes=56 << 20
        ),
        name="sage",
    )(features, w_self, w_neigh, bias.reshape(1, HID), cotangent, edge_src, edge_dst, edge_count)
    return hidden, feature_grad, grad_self, grad_neigh, grad_bias.reshape(HID)


def solution(mesh):
    rows = P(("group", "member"), None)
    return jax.shard_map(
        on_device,
        mesh=mesh,
        in_specs=(rows, P(), P(), P(), rows, rows, rows, P(("group", "member"))),
        out_specs=(rows, rows, P(), P(), P()),
        check_vma=False,
    )
```

time: 915 us -> 112 us (0.12)
  waiting for transfers between devices: 532 us -> 0 us
  blocking collectives: 305 us -> 0 us
  Pallas kernels: 0 us -> 106 us
  other arithmetic: 47.3 us -> 0 us
  between operations: 14.6 us -> 1.31 us
    psum x1 -> x0, waiting for transfers between devices: 352 us -> none  [on_device(): lax.psum((self_part, neigh_part, bias_part, hub_part), ('group', 'member'))]
    psum x2 -> x0, blocking collectives: 192 us -> none  [the longest x1 103 us: on_device(): lax.psum((self_part, neigh_part, bias_part, hub_part), ('group', 'member'))]
    all_gather x1 -> x0, blocking collectives: 113 us -> none  [on_device(): lax.all_gather(features[:HUB_DEV], ('group', 'member'), axis=0, tiled=True)]
    reduce_scatter x2 -> x0, waiting for transfers between devices: 110 us -> none  [the longest x1 103 us: on_device(): lax.psum_scatter(source_part[:group_rows], 'member', scatter_dimension=0,...]
    pallas_call x0 -> x1, Pallas kernels: none -> 106 us  [on_device(): pl.pallas_call(kernel, out_shape=(jax.ShapeDtypeStruct((ROWS, HID), f32),...]
    all_gather x2 -> x0, waiting for transfers between devices: 69.5 us -> none  [fetch_rows(): gathered = lax.all_gather(values_in, 'member', axis=0, tiled=True)]
    scatter-add x3 -> x0, other arithmetic: 42 us -> none  [the longest x1 23.3 us: on_device(): jax.ops.segment_sum(neighbour, target, num_segments=group_rows)]
  transfers between devices with their start and end apart: 5 -> 0, of which waited for: 4 -> 0; matrix products, arithmetic and copies ran while one was open for 2% -> 0% of each run, Pallas kernels for 0% -> 0%
where the time goes in v1:
time: 112 us
  Pallas kernels  106 us (95%)
  local copies, waits for them, and re-layouts  4.42 us (4%)
  between operations  1.31 us (1%)
    pallas_call x1, Pallas kernels, on_device(): pl.pallas_call(kernel, out_shape=(jax.ShapeDtypeStruct((ROWS, HID), f32),...  106 us
    unnamed x13, local copies, waits for them, and re-layouts  4.42 us

profile of v1, /device:TPU:1, one launch (start us, length us, event | category | flops | bytes accessed | tf_op | source)
XLA Modules:
  0.0 111.6 jit_solution(11767267631729144256)
XLA Ops:
  1.3 105.8 %sage.1 = (f32[128,256]{1,0:T(8,128)}, f32[128,128]{1,0:T(8,128)}, f32[128,256]{1,0:T(8,128)}, f32[128,256]{1,0:T(8,128)}, f32[1,256]{1,0:T(1,128)}) custom-call(f32[128,128]{1,0:T(8,128)} %feat.1, f32[128,256]{1,0:T(8,128)} %w_self.1, f32[128,256]{1,0:T(8,128)} %w_neigh.1, f32[1,256]{1,0:T(1,128)} %bitcast.2, f32[128,256]{1,0:T(8,128)} %cot.1, ...), custom_call_target="tpu_custom_call" | custom-call | tf_op jit(solution)/shard_map/sage/pallas_call | solution.py:380
  107.1 0.0 copy-start.2
  107.1 0.0 copy-start.1
  107.1 1.6 %copy.19 = f32[128,256]{1,0:T(8,128)} copy(f32[128,256]{1,0:T(8,128)} %get-tuple-element.20) | data formatting | bytes 262144
  108.8 0.0 copy-done.2
  108.8 0.6 copy.20
  109.4 0.0 copy-done.1
  109.4 0.0 copy-start
  109.4 0.7 copy.21
  110.0 0.3 copy-done
  110.3 0.0 copy-start.3
  110.3 0.7 copy.22
  111.0 0.0 copy-done.3
  111.0 0.6 copy.23
Async XLA Ops:
  107.1 1.6 %copy-start.2 = (f32[128,128]{1,0:T(8,128)S(1)}, f32[128,128]{1,0:T(8,128)}, u32[]{:S(2)}) copy-start(f32[128,128]{1,0:T(8,128)} %get-tuple-element.21) | copy-start | bytes 196612
  107.1 2.3 %copy-start.1 = (f32[128,256]{1,0:T(8,128)S(1)}, f32[128,256]{1,0:T(8,128)}, u32[]{:S(2)}) copy-start(f32[128,256]{1,0:T(8,128)} %get-tuple-element.22) | copy-start | bytes 393220
  109.4 1.0 copy-start
  110.3 0.7 copy-start.3

commit v2 on v1

v2 whole, which is shorter than its diff:
```python
import jax
import jax.numpy as jnp
from jax import lax
from jax.experimental import pallas as pl
from jax.experimental.pallas import tpu as pltpu
from jax.sharding import PartitionSpec as P

f32, bf16, i32 = jnp.float32, jnp.bfloat16, jnp.int32
MESH = pl.DeviceIdType.MESH
G, M = 16, 32
ROWS = 128
IN, HID = 128, 256
CHUNK = 1024
LOCAL = M * ROWS
LO = 256
HI_V = LOCAL // LO
HI_S = HI_V + G * M // LO
N = 2
NT = (((1,), (1,)), ((), ()))


def dot(a, b, dims=(((1,), (0,)), ((), ()))):
    return lax.dot_general(a, b, dims, precision=lax.Precision.HIGHEST, preferred_element_type=f32)


def split8(x):
    high = x.astype(bf16).astype(f32)
    return jnp.concatenate([high, x - high], axis=0)


def fold8(x):
    return x + pltpu.roll(x, 4, 0)


def far_first(k, n):
    k = n - k
    odd = lax.rem(k, 2)
    return odd * ((k + 1) // 2) + (1 - odd) * (n - k // 2)


def lane_blocks():
    return lax.broadcasted_iota(i32, (8, 128), 1) >> 4, lax.broadcasted_iota(i32, (8, 128), 0)


def turned(x, rows):
    block, sub = lane_blocks()
    aligned = x
    for k in range(1, 8):
        aligned = jnp.where(sub == k, pltpu.roll(x, 16 * k, 1), aligned)
    out = []
    for c in range(rows):
        moved = pltpu.roll(aligned, 128 - 16 * c, 1) if c else aligned
        out.append(jnp.sum(jnp.where(block == sub, moved, 0.0), axis=0, keepdims=True))
    return out


def kernel(
    feat_h, w_self_h, w_neigh_h, bias_h, cot_h, src_h, dst_h, cnt_h,
    hid_o, fg_o, gs_o, gn_o, gb_o,
    feat, w_self, w_neigh, bias, cot, e_src, e_dst, e_cnt, hid, fg, gb,
    va, vb, acc, tab, hub_t,
    hubrx, erx, fts, frx, hts, hrx, sums, sumrx, mgs, mgrx,
    g1s, g1rx, p2s, p2rx, p3s, p3rx, p4s, p4rx,
    bs, brx, hbs, hbrx, h2s, h2rx,
    ssem, rsem, esem, isem, osem,
):
    g, m = lax.axis_index("group"), lax.axis_index("member")
    core, z = lax.rem(m, 2), m // 2
    sib = m + 1 - 2 * core
    sub16 = lax.broadcasted_iota(i32, (16, 128), 0)
    iota16 = sub16.astype(f32).astype(bf16)
    pat16 = (sub16 // 8).astype(f32).astype(bf16)
    one16 = jnp.ones((16, 128), bf16)
    zero16 = jnp.zeros((16, 128), bf16)

    barrier = pltpu.get_barrier_semaphore()

    @pl.loop(1, M)
    def _(step):
        to = lax.rem(m + far_first(step, M), M)
        pl.semaphore_signal(barrier, inc=1, device_id=(g, to), device_id_type=MESH)

    @pl.loop(1, G)
    def _(step):
        pl.semaphore_signal(barrier, inc=1, device_id=(lax.rem(g + step, G), m), device_id_type=MESH)

    fetches = [
        pltpu.make_async_copy(a, b, isem.at[k])
        for k, (a, b) in enumerate(
            [
                (feat_h, feat), (src_h, e_src), (dst_h, e_dst), (cnt_h, e_cnt),
                (w_self_h, w_self), (bias_h, bias), (w_neigh_h, w_neigh), (cot_h, cot),
            ]
        )
    ]
    for fetch in fetches:
        fetch.start()

    def copy_to(src, dst, k, gg, mm, recv=None):
        return pltpu.make_async_remote_copy(
            src_ref=src, dst_ref=dst, send_sem=ssem.at[k],
            recv_sem=rsem.at[k] if recv is None else recv,
            device_id=(gg, mm), device_id_type=MESH,
        )

    def over_members(src, dst, k):
        @pl.loop(1, M)
        def _(step):
            to = lax.rem(m + far_first(step, M), M)
            copy_to(src.at[to], dst.at[m], k, g, to).start()
        dst[m] = src[m]

    def over_groups(src, dst, k):
        @pl.loop(1, G)
        def _(step):
            to = lax.rem(g + step, G)
            copy_to(src.at[to], dst.at[g], k, to, m).start()
        dst[g] = src[g]

    def wait(buf, n, sem):
        view = buf.at[pl.ds(0, n)]
        pltpu.make_async_copy(view, view, sem).wait()

    def arrive(name, buf, n, k):
        with jax.named_scope(name):
            wait(buf, n, rsem.at[k])

    def rows4(dst, x):
        for i in range(M):
            dst[i] = x[4 * i : 4 * i + 4, :]

    def joined(src):
        return jnp.concatenate([src[i] for i in range(M)], axis=0)

    def stacked(src):
        return jnp.concatenate([src[i] for i in range(M)], axis=0)

    for k in range(4):
        fetches[k].wait()
    with jax.named_scope("pack"):
        ft = feat[...].T
        rows4(fts, ft)
        src = e_src[...]
        hub = src - LOCAL
        src = jnp.where(hub >= 0, LOCAL + ((hub & (M - 1)) * G + (hub >> 5)), src)
        used = lax.broadcasted_iota(i32, (1, CHUNK), 1) < e_cnt[...]
        dst = jnp.where(used, e_dst[...], LOCAL)
        for r in range(8):
            erx[m, r : r + 1, :] = src[:, 128 * r : 128 * r + 128]
            erx[m, 8 + r : 9 + r, :] = dst[:, 128 * r : 128 * r + 128]

    with jax.named_scope("entry_wait"):
        pl.semaphore_wait(barrier, M - 1 + G - 1)

    hub_tile = feat.at[pl.ds(0, 8)]

    @pl.loop(1, G)
    def _(step):
        copy_to(hub_tile, hubrx.at[g], 0, lax.rem(g + step, G), m).start()

    hubrx[g] = feat[0:8, :]
    copy_to(erx.at[m], erx.at[m], 1, g, sib, esem.at[m]).start()

    @pl.loop(1, M // 2)
    def _(step):
        to = lax.rem(z + far_first(step, M // 2), M // 2) * 2 + core
        copy_to(erx.at[m], erx.at[m], 1, g, to, esem.at[m]).start()

    over_members(fts, frx, 2)
    for k in range(4, 6):
        fetches[k].wait()
    self_act = dot(feat[...], w_self[...]) + bias[...]
    for k in range(6, 8):
        fetches[k].wait()

    arrive("hub_wait", hubrx, G - 1, 0)
    with jax.named_scope("hub_pack"):
        hub_rows = jnp.concatenate(
            [hubrx[i][0:1, :] for i in range(G)] + [jnp.zeros((128 - G, 128), f32)], axis=0
        )
        hub_t[...] = hub_rows.T
        packed = hub_t[pl.ds(0, M, stride=4), :]
        for c in range(1, 4):
            packed = packed + pltpu.roll(hub_t[pl.ds(c, M, stride=4), :], 16 * c, 1)
        for i in range(M):
            hts[i] = packed[i : i + 1, :]
        over_members(hts, hrx, 3)

    def edge_wait(slot):
        pltpu.make_async_copy(erx.at[slot], erx.at[slot], esem.at[slot]).wait()

    def nth_chip(step):
        return lax.rem(z + M // 2 - far_first(M // 2 - step, M // 2), M // 2) * 2

    with jax.named_scope("edges"):
        @pl.loop(1, M // 2)
        def _(step):
            slot = nth_chip(step) + core
            edge_wait(slot)
            copy_to(erx.at[slot], erx.at[slot], 1, g, sib, esem.at[slot]).start()

        edge_wait(sib)

        @pl.loop(1, M // 2)
        def _(step):
            edge_wait(nth_chip(step) + 1 - core)

    def table(src):
        for t in range(HI_V // 2):
            for c in range(2):
                tab[16 * t : 16 * t + 16, 128 * c : 128 * c + 128] = jnp.concatenate(
                    [split8(src[4 * t + c]), split8(src[4 * t + 2 + c])], axis=0
                ).astype(bf16)

    def spread_row(row, pattern):
        return jnp.broadcast_to(row.astype(f32), (16, 128)).astype(bf16) - pattern

    def hots(low, q):
        halves = []
        for r in (2 * q, 2 * q + 1):
            row = spread_row(low[r : r + 1, :], iota16)
            halves.append(
                jnp.concatenate(
                    [jnp.where(row == jnp.array(16 * t, bf16), one16, zero16) for t in range(LO // 16)], axis=0
                )
            )
        return jnp.concatenate(halves, axis=1)

    def aggregate(forward, between):
        n_in, n_out = (HI_S, HI_V) if forward else (HI_V, HI_S)
        i_at, o_at = (0, 8) if forward else (8, 0)

        def gather(j, v, k):
            ins, outs = erx[j, i_at : i_at + 8, :], erx[j, o_at : o_at + 8, :]
            in_lo, in_hi, out_hi = ins & (LO - 1), ins >> 8, outs >> 8
            for q in range(4):
                rows = jnp.dot(tab[0 : 8 * n_in, :], hots(in_lo, q), preferred_element_type=f32)
                for c in range(2):
                    r = 2 * q + c
                    cols = slice(128 * c, 128 * c + 128)
                    high = jnp.broadcast_to(in_hi[r : r + 1, :], (8, 128))
                    w = jnp.zeros((8, 128), f32)
                    for h in range(n_in):
                        w = jnp.where(high == h, rows[8 * h : 8 * h + 8, cols], w)
                    w16 = jnp.concatenate([w, w], axis=0).astype(bf16)
                    row = spread_row(out_hi[r : r + 1, :], pat16)
                    for t in range(n_out // 2):
                        v[4 * k + q, 16 * t : 16 * t + 16, cols] = jnp.where(
                            row == jnp.array(2 * t, bf16), w16, zero16
                        )
                    if forward:
                        mine = jnp.broadcast_to(out_hi[r : r + 1, :], (16, 128)) == z
                        v[4 * k + q, 8 * n_out : 8 * n_out + 16, cols] = jnp.where(
                            mine & (sub16 == 0), jnp.float32(1), jnp.float32(0)
                        ).astype(bf16)

        def scatter(j, v):
            total = None
            for k in range(N):
                out_lo = erx[j + k, o_at : o_at + 8, :] & (LO - 1)
                for q in range(4):
                    part = lax.dot_general(hots(out_lo, q), v[4 * k + q], NT, preferred_element_type=f32)
                    total = part if total is None else total + part
            acc[...] += total

        def step(i):
            j = 2 * N * i
            scatter(jnp.maximum(j - N, 0), vb)
            for k in range(N):
                gather(j + k, va, k)
            scatter(j, va)
            for k in range(N):
                gather(j + N + k, vb, k)

        acc[...] = jnp.zeros_like(acc)
        vb[...] = jnp.zeros_like(vb)
        steps, done = M // (2 * N), 0
        for until, action in between + [(steps, None)]:
            pl.loop(done, until)(step)
            done = until
            if action is not None:
                action()
        scatter(M - N, vb)
        last = jnp.concatenate([acc[:, 128:144], jnp.zeros((LO, 112), f32)], axis=1)
        return acc[:, 0:128].T, last.T[0:16, :]

    def unpack(dst, total):
        for h in range(HI_V):
            both = fold8(total[8 * h : 8 * h + 8, :])
            dst[2 * h] = both[0:4, 0:128]
            dst[2 * h + 1] = both[0:4, 128:256]

    arrive("feat_wait", frx, M - 1, 2)
    with jax.named_scope("table"):
        table(frx)
    arrive("hubcol_wait", hrx, M - 1, 3)
    with jax.named_scope("hub_table"):
        arrived = stacked(hrx)
        quarter = [jnp.concatenate(turned(arrived[8 * q : 8 * q + 8, :], 4), axis=0) for q in range(4)]
        for c in range(2):
            tab[8 * HI_V : 8 * HI_S, 128 * c : 128 * c + 128] = jnp.concatenate(
                [split8(quarter[c]), split8(quarter[2 + c])], axis=0
            ).astype(bf16)
    with jax.named_scope("forward"):
        total, own = aggregate(True, [])
    with jax.named_scope("sums"):
        unpack(sums, total)
        over_members(sums, sumrx, 4)
        degree = jnp.where(core == 0, own[0:1, 0:128], own[0:1, 128:256])
        inverse = 1.0 / jnp.maximum(degree, 1.0)
        arrive("sum_wait", sumrx, M - 1, 4)
    with jax.named_scope("dense"):
        mean_t = joined(sumrx) * inverse
        pre_act = self_act + dot(mean_t.T, w_neigh[...])
        sig = jax.nn.sigmoid(pre_act)
        pre_grad = cot[...] * sig * (1.0 + pre_act * (1.0 - sig))
        rows4(mgs, dot(w_neigh[...], pre_grad, NT) * inverse)
        over_members(mgs, mgrx, 5)
    with jax.named_scope("weight_grads"):
        hid[...] = pre_act * sig
        hid_out = pltpu.make_async_copy(hid, hid_o, osem.at[0])
        hid_out.start()
        grad_s = dot(ft, pre_grad)
        grad_n = dot(mean_t, pre_grad)
        grad_b = jnp.broadcast_to(jnp.sum(pre_grad, axis=0, keepdims=True), (8, HID))
        for p in range(G):
            half = grad_s if p < G // 2 else grad_n
            at = 16 * (p % (G // 2))
            g1s[p, 0:16, :] = half[at : at + 16, :]
            g1s[p, 16:24, :] = grad_b
        over_groups(g1s, g1rx, 6)
        fg[...] = dot(pre_grad, w_self[...], NT)

    scale = 1.0 / (float(G * M * ROWS) ** 0.5)

    def reduce_groups():
        arrive("p1_wait", g1rx, G - 1, 6)
        total = g1rx[0]
        for i in range(1, G):
            total = total + g1rx[i]
        b0, b1 = total[16:17, 0:128], total[16:17, 128:256]
        rest = jnp.concatenate([b0, b1, jnp.zeros((1, 128), f32)], axis=0)
        for i in range(M):
            c = 128 * (i % 2)
            p2s[i] = jnp.concatenate([total[i // 2 : i // 2 + 1, c : c + 128], rest], axis=0)
        over_members(p2s, p2rx, 7)

    def reduce_members():
        arrive("p2_wait", p2rx, M - 1, 7)
        total = p2rx[0]
        for i in range(1, M):
            total = total + p2rx[i]
        total = total * scale
        gb[:, 0:128] = total[1:2, :]
        gb[:, 128:256] = total[2:3, :]
        p3s[...] = total[0:1, :]

        @pl.loop(1, M)
        def _(step):
            copy_to(p3s, p3rx.at[m], 8, g, lax.rem(m + far_first(step, M), M)).start()

        p3rx[m] = p3s[...]

    def collect_members():
        arrive("p3_wait", p3rx, M - 1, 8)
        for i in range(M):
            c = 128 * (i % 2)
            p4s[i // 2 : i // 2 + 1, c : c + 128] = p3rx[i]

        @pl.loop(1, G)
        def _(step):
            copy_to(p4s, p4rx.at[g], 9, lax.rem(g + step, G), m).start()

        p4rx[g] = p4s[...]

    arrive("mean_wait", mgrx, M - 1, 5)
    with jax.named_scope("backward"):
        table(mgrx)
        total, hubs = aggregate(False, [(M // (16 * N), reduce_groups), (7 * M // (16 * N), reduce_members)])
    with jax.named_scope("tail"):
        for q in range(4):
            part = fold8(hubs[8 * (q // 2) : 8 * (q // 2) + 8, 128 * (q % 2) : 128 * (q % 2) + 128])
            for k, row in enumerate(turned(part, 8)):
                hbs[8 * q + k] = row
        over_members(hbs, hbrx, 10)
        unpack(bs, total)
        over_members(bs, brx, 11)
        collect_members()
        arrive("hubgrad_wait", hbrx, M - 1, 10)
        got = jnp.concatenate([stacked(hbrx), jnp.zeros((128 - M, 128), f32)], axis=0).T
        rows = got[0:16, :]
        for c in range(1, 4):
            rows = rows + pltpu.roll(got[16 * c : 16 * c + 16, :], 32 * c, 1)
        for p in range(G):
            h2s[p] = rows[p : p + 1, :]
        over_groups(h2s, h2rx, 12)
        arrive("grad_wait", brx, M - 1, 11)
        fg[...] += joined(brx).T
        arrive("p4_wait", p4rx, G - 1, 9)
        late = [
            pltpu.make_async_copy(p4rx.at[pl.ds(0, G // 2)], gs_o, osem.at[1]),
            pltpu.make_async_copy(p4rx.at[pl.ds(G // 2, G // 2)], gn_o, osem.at[2]),
            pltpu.make_async_copy(gb, gb_o, osem.at[3]),
        ]
        for copy in late:
            copy.start()
        arrive("hubsum_wait", h2rx, G - 1, 12)
        total = h2rx[0]
        for i in range(1, G):
            total = total + h2rx[i]
        lane = lax.broadcasted_iota(i32, (128, 128), 0)
        feature = lax.broadcasted_iota(i32, (128, 128), 1)
        order = jnp.where((lane & 31) * 4 + (lane >> 5) == feature, jnp.float32(1), jnp.float32(0))
        first = lax.broadcasted_iota(i32, (8, 128), 0) == 0
        total = jnp.where(first, jnp.broadcast_to(total, (8, 128)), 0.0)
        fg[0:8, :] += dot(total, order)
        fg_out = pltpu.make_async_copy(fg, fg_o, osem.at[4])
        fg_out.start()

    for buf, n, k in (
        (hubrx, G, 0), (erx, M, 1), (frx, M, 2), (hrx, M, 3), (sumrx, M, 4), (mgrx, M, 5), (g1rx, G, 6),
        (p2rx, M, 7), (p3rx, M, 8), (p4rx, G, 9), (hbrx, M, 10), (brx, M, 11), (h2rx, G, 12),
    ):
        wait(buf, n - 1, ssem.at[k])
    for copy in [hid_out] + late + [fg_out]:
        copy.wait()


def write_out(*refs):
    for a, b in zip(refs[:5], refs[5:]):
        b[...] = a[...]


def on_device(features, w_self, w_neigh, bias, cotangent, edge_src, edge_dst, edge_count):
    anywhere, vmem = pl.BlockSpec(memory_space=pl.ANY), pl.BlockSpec(memory_space=pltpu.VMEM)
    quads = pltpu.VMEM((M, 4, 128), f32)
    lines = pltpu.VMEM((M, 1, 128), f32)
    args = [features, w_self, w_neigh, bias.reshape(1, HID), cotangent, edge_src, edge_dst, edge_count.reshape(1, 1)]
    scratch = [pltpu.VMEM(a.shape, a.dtype) for a in args] + [
        pltpu.VMEM((ROWS, HID), f32), pltpu.VMEM((ROWS, IN), f32), pltpu.VMEM((1, HID), f32),
        pltpu.VMEM((4 * N, 8 * HI_S, 256), bf16), pltpu.VMEM((4 * N, 8 * HI_S, 256), bf16),
        pltpu.VMEM((LO, 8 * HI_S), f32), pltpu.VMEM((8 * HI_S, LO), bf16), pltpu.VMEM((128, 128), f32),
        pltpu.VMEM((G, 8, 128), f32), pltpu.VMEM((M, 16, 128), i32),
        quads, quads, lines, lines, quads, quads, quads, quads,
        pltpu.VMEM((G, 24, HID), f32), pltpu.VMEM((G, 24, HID), f32), quads, quads,
        pltpu.VMEM((1, 128), f32), lines, pltpu.VMEM((16, HID), f32), pltpu.VMEM((G, 16, HID), f32),
        quads, quads, lines, lines, pltpu.VMEM((G, 1, 128), f32), pltpu.VMEM((G, 1, 128), f32),
        pltpu.SemaphoreType.DMA((13,)), pltpu.SemaphoreType.DMA((13,)), pltpu.SemaphoreType.DMA((M,)),
        pltpu.SemaphoreType.DMA((8,)), pltpu.SemaphoreType.DMA((5,)),
    ]
    shapes = [(ROWS, HID), (ROWS, IN), (G // 2, 16, HID), (G // 2, 16, HID), (1, HID)]
    results = pl.pallas_call(
        kernel,
        out_shape=[jax.ShapeDtypeStruct(s, f32) for s in shapes],
        in_specs=[anywhere] * 8,
        out_specs=[anywhere] * 5,
        scratch_shapes=scratch,
        compiler_params=pltpu.CompilerParams(
            collective_id=0, has_side_effects=True, vmem_limit_bytes=56 << 20
        ),
        name="sage",
    )(*args)
    final = [(ROWS, HID), (ROWS, IN), (IN, HID), (IN, HID), (1, HID)]
    results = pl.pallas_call(
        write_out,
        out_shape=[jax.ShapeDtypeStruct(s, f32) for s in final],
        in_specs=[vmem] * 5,
        out_specs=[vmem] * 5,
        name="write_out",
    )(*[r.reshape(s) for r, s in zip(results, final)])
    return (*results[:4], results[4].reshape(HID))


def solution(mesh):
    rows = P(("group", "member"), None)
    return jax.shard_map(
        on_device,
        mesh=mesh,
        in_specs=(rows, P(), P(), P(), rows, rows, rows, P(("group", "member"))),
        out_specs=(rows, rows, P(), P(), P()),
        check_vma=False,
    )
```

time: 112 us -> 84.3 us (0.75)
  Pallas kernels: 106 us -> 82.9 us
  local copies, waits for them, and re-layouts: 4.42 us -> 0 us
    pallas_call x1 -> x2, Pallas kernels: 106 us -> 82.9 us  [the longest x1 81 us: on_device(): pl.pallas_call(kernel, out_shape=[jax.ShapeDtypeStruct(s, f32) for s in s...]
    unnamed x13 -> x0, local copies, waits for them, and re-layouts: 4.42 us -> none
where the time goes in v2:
time: 84.3 us; the launch traced here: 84.2 us
  Pallas kernels  82.9 us (98%)
  between operations  1.29 us (2%)
    pallas_call x1, Pallas kernels, on_device(): pl.pallas_call(kernel, out_shape=[jax.ShapeDtypeStruct(s, f32) for s in s...  81 us
    pallas_call x1, Pallas kernels, on_device(): pl.pallas_call(write_out, out_shape=[jax.ShapeDtypeStruct(s, f32) for s i...  1.84 us

profile of v2, /device:TPU:1, one launch (start us, length us, event | category | flops | bytes accessed | tf_op | source)
XLA Modules:
  0.0 84.2 jit_solution(14804235013882056684)
XLA Ops:
  1.3 81.0 %sage.1 = (f32[128,256]{1,0:T(8,128)}, f32[128,128]{1,0:T(8,128)}, f32[8,16,256]{2,1,0:T(8,128)}, f32[8,16,256]{2,1,0:T(8,128)}, f32[1,256]{1,0:T(1,128)}) custom-call(f32[128,128]{1,0:T(8,128)} %feat_h.1, f32[128,256]{1,0:T(8,128)} %w_self_h.1, f32[128,256]{1,0:T(8,128)} %w_neigh_h.1, f32[1,256]{1,0:T(1,128)} %bitcast.8, f32[128,256]{1,0:T(8,128)} %cot_h.1, ...), custom_call_target="tpu_custom_call" | custom-call | tf_op jit(solution)/shard_map/sage/pallas_call | solution.py:452
  82.3 1.8 %write_out.1 = (f32[128,256]{1,0:T(8,128)}, f32[128,128]{1,0:T(8,128)}, f32[128,256]{1,0:T(8,128)}, f32[128,256]{1,0:T(8,128)}, f32[1,256]{1,0:T(1,128)}) custom-call(f32[128,256]{1,0:T(8,128)} %get-tuple-element.15.refs_0_, f32[128,128]{1,0:T(8,128)} %get-tuple-element.16.refs_1_, f32[128,256]{1,0:T(8,128)} %bitcast.6, f32[128,256]{1,0:T(8,128)} %bitcast.7, ...), custom_call_target="tpu_custom_call" | custom-call | tf_op jit(solution)/shard_map/write_out/pallas_call | solution.py:464

commit v3 on v2

v3 whole, which is shorter than its diff:
```python
import jax
import jax.numpy as jnp
from jax import lax
from jax.experimental import pallas as pl
from jax.experimental.pallas import tpu as pltpu
from jax.sharding import PartitionSpec as P

f32, bf16, i32 = jnp.float32, jnp.bfloat16, jnp.int32
MESH = pl.DeviceIdType.MESH
G, M = 16, 32
ROWS = 128
IN, HID = 128, 256
CHUNK = 1024
LOCAL = M * ROWS
LO = 256
HI_V = LOCAL // LO
HI_H = G * M // LO
N = 4
NT = (((1,), (1,)), ((), ()))


def halves(x):
    high = x.astype(bf16)
    return high, (x - high.astype(f32)).astype(bf16)


def dot(a, b, dims=(((1,), (0,)), ((), ()))):
    (a0, a1), (b0, b1) = halves(a), halves(b)

    def part(x, y):
        return lax.dot_general(x, y, dims, preferred_element_type=f32)

    return part(a0, b0) + (part(a0, b1) + part(a1, b0))


def split8(x):
    high = x.astype(bf16).astype(f32)
    return jnp.concatenate([high, x - high], axis=0)


def fold8(x):
    return x + pltpu.roll(x, 4, 0)


def each_far_first(me, n, send):
    send(lax.rem(me + n // 2, n))

    @pl.loop(1, n // 2)
    def _(near):
        send(lax.rem(me + n // 2 + near, n))
        send(lax.rem(me + n // 2 - near, n))


def kernel(
    feat_h, w_self_h, w_neigh_h, bias_h, cot_h, src_h, dst_h, cnt_h,
    hid_o, fg_o, gs_o, gn_o, gb_o,
    feat, w_self, w_neigh, bias, cot, e_src, e_dst, e_cnt, hid, fg, gb,
    va, vb, acc, tab, own,
    hubs, hub_rows, erx, fts, frx, sums, sumrx, mgs, mgrx,
    g1s, g1rx, p2s, p2rx, p3s, p3rx, p4s, p4rx,
    bs, brx, hgs, hgrx, h2s, h2rx,
    ssem, rsem, esem, isem, osem,
):
    g, m = lax.axis_index("group"), lax.axis_index("member")
    core, z = lax.rem(m, 2), m // 2
    sib = m + 1 - 2 * core
    sub16 = lax.broadcasted_iota(i32, (16, 128), 0)
    iota16 = sub16.astype(f32).astype(bf16)
    pat16 = (sub16 // 8).astype(f32).astype(bf16)
    one16 = jnp.ones((16, 128), bf16)
    zero16 = jnp.zeros((16, 128), bf16)

    barrier = pltpu.get_barrier_semaphore()
    with jax.named_scope("greet"):

        def greet(to):
            pl.semaphore_signal(barrier, inc=1, device_id=(g, to), device_id_type=MESH)

        each_far_first(m, M, greet)

        @pl.loop(1, G)
        def _(step):
            pl.semaphore_signal(barrier, inc=1, device_id=(lax.rem(g + step, G), m), device_id_type=MESH)

    fetches = [
        pltpu.make_async_copy(a, b, isem.at[k])
        for k, (a, b) in enumerate(
            [
                (feat_h, feat), (src_h, e_src), (dst_h, e_dst), (cnt_h, e_cnt),
                (w_self_h, w_self), (bias_h, bias), (w_neigh_h, w_neigh), (cot_h, cot),
            ]
        )
    ]
    for fetch in fetches:
        fetch.start()

    def copy_to(src, dst, k, gg, mm, recv=None):
        return pltpu.make_async_remote_copy(
            src_ref=src, dst_ref=dst, send_sem=ssem.at[k],
            recv_sem=rsem.at[k] if recv is None else recv,
            device_id=(gg, mm), device_id_type=MESH,
        )

    def over_members(src, dst, k):
        each_far_first(m, M, lambda to: copy_to(src.at[to], dst.at[m], k, g, to).start())
        dst[m] = src[m]

    def to_members(src, dst, k):
        each_far_first(m, M, lambda to: copy_to(src, dst.at[m], k, g, to).start())

    def over_groups(src, dst, k):
        @pl.loop(1, G)
        def _(step):
            to = lax.rem(g + step, G)
            copy_to(src.at[to], dst.at[g], k, to, m).start()
        dst[g] = src[g]

    def wait(buf, n, sem):
        view = buf.at[pl.ds(0, n)]
        pltpu.make_async_copy(view, view, sem).wait()

    def arrive(name, buf, n, k):
        with jax.named_scope(name):
            wait(buf, n, rsem.at[k])

    def rows4(dst, x):
        for i in range(M):
            dst[i] = x[4 * i : 4 * i + 4, :]

    def joined(src):
        return jnp.concatenate([src[i] for i in range(M)], axis=0)

    for k in range(4):
        fetches[k].wait()
    with jax.named_scope("pack"):
        ft = feat[...].T
        rows4(fts, ft)
        src = e_src[...]
        used = lax.broadcasted_iota(i32, (1, CHUNK), 1) < e_cnt[...]
        dst = jnp.where(used, e_dst[...], LOCAL)
        for r in range(8):
            erx[m, r : r + 1, :] = src[:, 128 * r : 128 * r + 128]
            erx[m, 8 + r : 9 + r, :] = dst[:, 128 * r : 128 * r + 128]

    with jax.named_scope("entry_wait"):
        pl.semaphore_wait(barrier, M - 1 + G - 1)

    hubs[m] = feat[0:1, :]
    to_members(hubs.at[m], hubs, 0)
    over_members(fts, frx, 2)

    def edge_wait(slot):
        pltpu.make_async_copy(erx.at[slot], erx.at[slot], esem.at[slot]).wait()

    def edge_send(slot, to):
        copy_to(erx.at[slot], erx.at[slot], 1, g, to, esem.at[slot]).start()

    edge_send(m, sib)

    def nth_slot(n, other):
        odd = lax.rem(n, 2)
        ahead = odd * ((n + 1) // 2) + (1 - odd) * (M // 2 - n // 2)
        return lax.rem(z + ahead, M // 2) * 2 + (1 - core if other else core)

    @pl.loop(1, M // 2)
    def _(n):
        edge_send(m, nth_slot(n, False))

    def hand_on(quarter):
        @pl.loop(0, 4)
        def _(k):
            slot = nth_slot(4 * quarter + k, False)
            edge_wait(slot)
            edge_send(slot, sib)

    def others(quarter):
        @pl.loop(0, 4)
        def _(k):
            edge_wait(nth_slot(4 * quarter + k, True))

    with jax.named_scope("edges_first"):
        @pl.loop(1, 4)
        def _(k):
            slot = nth_slot(k, False)
            edge_wait(slot)
            edge_send(slot, sib)

    def table(src):
        for t in range(HI_V // 2):
            for c in range(2):
                tab[16 * t : 16 * t + 16, 128 * c : 128 * c + 128] = jnp.concatenate(
                    [split8(src[4 * t + c]), split8(src[4 * t + 2 + c])], axis=0
                ).astype(bf16)

    def spread_row(row, pattern):
        return jnp.broadcast_to(row.astype(f32), (16, 128)).astype(bf16) - pattern

    def hots(low, q):
        halves = []
        for r in (2 * q, 2 * q + 1):
            row = spread_row(low[r : r + 1, :], iota16)
            halves.append(
                jnp.concatenate(
                    [jnp.where(row == jnp.array(16 * t, bf16), one16, zero16) for t in range(LO // 16)], axis=0
                )
            )
        return jnp.concatenate(halves, axis=1)

    def aggregate(forward, between):
        i_at, o_at = (0, 8) if forward else (8, 0)
        width = 8 * HI_V + (16 if forward else 0)

        def slot(c, k):
            return nth_slot(c // 2 + k // 2, k % 2 == 1)

        def gather(j, v, k):
            j = slot(j, k)
            ins, outs = erx[j, i_at : i_at + 8, :], erx[j, o_at : o_at + 8, :]
            in_lo, in_hi, out_hi = ins & (LO - 1), ins >> 8, outs >> 8
            for q in range(4):
                rows = jnp.dot(tab[...], hots(in_lo, q), preferred_element_type=f32)
                for c in range(2):
                    r = 2 * q + c
                    cols = slice(128 * c, 128 * c + 128)
                    high = jnp.broadcast_to(in_hi[r : r + 1, :], (8, 128))
                    w = jnp.zeros((8, 128), f32)
                    for h in range(HI_V):
                        w = jnp.where(high == h, rows[8 * h : 8 * h + 8, cols], w)
                    w16 = jnp.concatenate([w, w], axis=0).astype(bf16)
                    row = spread_row(out_hi[r : r + 1, :], pat16)
                    for t in range(HI_V // 2):
                        v[4 * k + q, 16 * t : 16 * t + 16, cols] = jnp.where(
                            row == jnp.array(2 * t, bf16), w16, zero16
                        )
                    if forward:
                        mine = jnp.broadcast_to(out_hi[r : r + 1, :], (16, 128)) == z
                        v[4 * k + q, 8 * HI_V : 8 * HI_V + 16, cols] = jnp.where(
                            mine & (sub16 == 0), jnp.float32(1), jnp.float32(0)
                        ).astype(bf16)

        def scatter(j, v):
            total = None
            for k in range(N):
                out_lo = erx[slot(j, k), o_at : o_at + 8, :] & (LO - 1)
                for q in range(4):
                    part = lax.dot_general(hots(out_lo, q), v[4 * k + q, 0:width, :], NT, preferred_element_type=f32)
                    total = part if total is None else total + part
            acc[:, 0:width] += total

        def step(i):
            j = 2 * N * i
            scatter(jnp.maximum(j - N, 0), vb)
            for k in range(N):
                gather(j, va, k)
            scatter(j, va)
            for k in range(N):
                gather(j + N, vb, k)

        acc[...] = jnp.zeros_like(acc)
        vb[...] = jnp.zeros_like(vb)
        @pl.loop(0, M // (2 * N))
        def _(i):
            between(i)
            step(i)

        scatter(M - N, vb)
        return acc[:, 0:128].T

    def unpack(dst, total):
        for h in range(HI_V):
            both = fold8(total[8 * h : 8 * h + 8, :])
            dst[2 * h] = both[0:4, 0:128]
            dst[2 * h + 1] = both[0:4, 128:256]

    arrive("feat_wait", frx, M - 1, 2)
    with jax.named_scope("table"):
        table(frx)
    arrive("hub_wait", hubs, M - 1, 0)

    @pl.loop(1, G)
    def _(step):
        copy_to(hubs, hub_rows.at[g], 3, lax.rem(g + step, G), m).start()

    hub_rows[g] = hubs[...]
    with jax.named_scope("forward"):
        def edges_in_time(i):
            pl.when(i < 3)(lambda: hand_on(i + 1))
            others(i)

        total = aggregate(True, edges_in_time)
    with jax.named_scope("sums"):
        unpack(sums, total)
        over_members(sums, sumrx, 4)
        last = jnp.concatenate([acc[:, 128:144], jnp.zeros((LO, 112), f32)], axis=1).T
        degree = jnp.where(core == 0, last[0:1, 0:128], last[0:1, 128:256])
        inverse = 1.0 / jnp.maximum(degree, 1.0)
        for k in range(4, 8):
            fetches[k].wait()
        self_act = dot(feat[...], w_self[...]) + bias[...]
    with jax.named_scope("own_hubs"):
        own[...] = jnp.zeros_like(own)

        @pl.loop(0, M // 4)
        def _(i):
            total = None
            for k in range(4):
                src, dst = erx[4 * i + k, 0:8, :], erx[4 * i + k, 8:16, :]
                hub = src - LOCAL
                key = jnp.where(
                    (hub >= 0) & ((dst >> 7) == m), ((hub >> 8) << 7) + (dst & (ROWS - 1)), -1
                )
                for q in range(4):
                    part = lax.dot_general(hots(src & (LO - 1), q), hots(key, q), NT, preferred_element_type=f32)
                    total = part if total is None else total + part
            own[...] += total

        arrive("hubrow_wait", hub_rows, G - 1, 3)
        from_hubs = jnp.zeros((IN, ROWS), f32)
        for h in range(HI_H):
            rows = jnp.concatenate([hub_rows[8 * h + p, i] for p in range(8) for i in range(M)], axis=0)
            from_hubs = from_hubs + dot(rows.T, own[:, ROWS * h : ROWS * h + ROWS])
    arrive("sum_wait", sumrx, M - 1, 4)
    with jax.named_scope("dense"):
        mean_t = (joined(sumrx) + from_hubs) * inverse
        pre_act = self_act + dot(mean_t.T, w_neigh[...])
        sig = jax.nn.sigmoid(pre_act)
        pre_grad = cot[...] * sig * (1.0 + pre_act * (1.0 - sig))
        grad_s = dot(ft, pre_grad)
        grad_n = dot(mean_t, pre_grad)
        for p in range(G):
            half = grad_s if p < G // 2 else grad_n
            at = 16 * (p % (G // 2))
            g1s[p] = half[at : at + 16, :]
        over_groups(g1s, g1rx, 6)
        mean_grad_t = dot(w_neigh[...], pre_grad, NT) * inverse
        rows4(mgs, mean_grad_t)
        over_members(mgs, mgrx, 5)
    with jax.named_scope("hub_grads"):
        grad_b = jnp.sum(pre_grad, axis=0, keepdims=True)
        grad_b = jnp.concatenate([grad_b[:, 0:128], grad_b[:, 128:256], jnp.zeros((6, 128), f32)], axis=0)
        for h in range(HI_H):
            part = dot(own[:, ROWS * h : ROWS * h + ROWS], mean_grad_t, NT)
            for p in range(8):
                hgs[8 * h + p, 0:M, :] = part[M * p : M * p + M, :]
                hgs[8 * h + p, M : M + 8, :] = grad_b
        over_groups(hgs, hgrx, 7)
        hid[...] = pre_act * sig
        hid_out = pltpu.make_async_copy(hid, hid_o, osem.at[0])
        hid_out.start()
        fg[...] = dot(pre_grad, w_self[...], NT)

    scale = 1.0 / (float(G * M * ROWS) ** 0.5)

    def summed(src, n):
        total = src[0]
        for i in range(1, n):
            total = total + src[i]
        return total

    def reduce_groups():
        arrive("p1_wait", g1rx, G - 1, 6)
        total = summed(g1rx, G)
        for i in range(M):
            c = 128 * (i % 2)
            p2s[i] = total[i // 2 : i // 2 + 1, c : c + 128]
        over_members(p2s, p2rx, 8)

    def reduce_hubs():
        arrive("hubgrad_wait", hgrx, G - 1, 7)
        total = summed(hgrx, G)
        rest = total[M : M + 3, :]
        for i in range(M):
            h2s[i] = jnp.concatenate([total[i : i + 1, :], rest], axis=0)
        over_members(h2s, h2rx, 9)

    def reduce_members():
        arrive("p2_wait", p2rx, M - 1, 8)
        p3s[...] = summed(p2rx, M) * scale
        to_members(p3s, p3rx, 10)
        p3rx[m] = p3s[...]

    def collect_members():
        arrive("p3_wait", p3rx, M - 1, 10)
        for i in range(M):
            c = 128 * (i % 2)
            p4s[i // 2 : i // 2 + 1, c : c + 128] = p3rx[i]

        @pl.loop(1, G)
        def _(step):
            copy_to(p4s, p4rx.at[g], 11, lax.rem(g + step, G), m).start()

        p4rx[g] = p4s[...]

    reduce_groups()
    arrive("mean_wait", mgrx, M - 1, 5)
    with jax.named_scope("backward"):
        table(mgrx)
        def reductions(i):
            pl.when(i == 1)(reduce_hubs)
            pl.when(i == 3)(reduce_members)

        total = aggregate(False, reductions)
    with jax.named_scope("tail"):
        unpack(bs, total)
        over_members(bs, brx, 12)
        arrive("hubsum_wait", h2rx, M - 1, 9)
        total = summed(h2rx, M)
        gb[:, 0:128] = total[1:2, :] * scale
        gb[:, 128:256] = total[2:3, :] * scale
        first = lax.broadcasted_iota(i32, (8, 128), 0) == 0
        fg[0:8, :] += jnp.where(first, jnp.broadcast_to(total[0:1, :], (8, 128)), 0.0)
        collect_members()
        arrive("grad_wait", brx, M - 1, 12)
        fg[...] += joined(brx).T
        late = [
            pltpu.make_async_copy(fg, fg_o, osem.at[1]),
            pltpu.make_async_copy(gb, gb_o, osem.at[2]),
            pltpu.make_async_copy(p4rx.at[pl.ds(0, G // 2)], gs_o, osem.at[3]),
            pltpu.make_async_copy(p4rx.at[pl.ds(G // 2, G // 2)], gn_o, osem.at[4]),
        ]
        for copy in late[0:2]:
            copy.start()
        arrive("p4_wait", p4rx, G - 1, 11)
        for copy in late[2:4]:
            copy.start()

    for buf, n, k in (
        (hubs, M, 0), (erx, M, 1), (frx, M, 2), (hub_rows, G, 3), (sumrx, M, 4), (mgrx, M, 5), (g1rx, G, 6),
        (hgrx, G, 7), (p2rx, M, 8), (h2rx, M, 9), (p3rx, M, 10), (p4rx, G, 11), (brx, M, 12),
    ):
        wait(buf, n - 1, ssem.at[k])
    for copy in [hid_out] + late:
        copy.wait()


def write_out(*refs):
    for a, b in zip(refs[:5], refs[5:]):
        b[...] = a[...]


def on_device(features, w_self, w_neigh, bias, cotangent, edge_src, edge_dst, edge_count):
    anywhere, vmem = pl.BlockSpec(memory_space=pl.ANY), pl.BlockSpec(memory_space=pltpu.VMEM)
    quads = pltpu.VMEM((M, 4, 128), f32)
    lines = pltpu.VMEM((M, 1, 128), f32)
    args = [features, w_self, w_neigh, bias.reshape(1, HID), cotangent, edge_src, edge_dst, edge_count.reshape(1, 1)]
    scratch = [pltpu.VMEM(a.shape, a.dtype) for a in args] + [
        pltpu.VMEM((ROWS, HID), f32), pltpu.VMEM((ROWS, IN), f32), pltpu.VMEM((1, HID), f32),
        pltpu.VMEM((4 * N, 8 * HI_V + 16, 256), bf16), pltpu.VMEM((4 * N, 8 * HI_V + 16, 256), bf16),
        pltpu.VMEM((LO, 8 * HI_V + 16), f32), pltpu.VMEM((8 * HI_V, LO), bf16),
        pltpu.VMEM((LO, HI_H * ROWS), f32),
        lines, pltpu.VMEM((G, M, 1, 128), f32), pltpu.VMEM((M, 16, 128), i32),
        quads, quads, quads, quads, quads, quads,
        pltpu.VMEM((G, 16, HID), f32), pltpu.VMEM((G, 16, HID), f32), lines, lines,
        pltpu.VMEM((1, 128), f32), lines, pltpu.VMEM((16, HID), f32), pltpu.VMEM((G, 16, HID), f32),
        quads, quads, pltpu.VMEM((G, M + 8, 128), f32), pltpu.VMEM((G, M + 8, 128), f32), quads, quads,
        pltpu.SemaphoreType.DMA((13,)), pltpu.SemaphoreType.DMA((13,)), pltpu.SemaphoreType.DMA((M,)),
        pltpu.SemaphoreType.DMA((8,)), pltpu.SemaphoreType.DMA((5,)),
    ]
    shapes = [(ROWS, HID), (ROWS, IN), (G // 2, 16, HID), (G // 2, 16, HID), (1, HID)]
    results = pl.pallas_call(
        kernel,
        out_shape=[jax.ShapeDtypeStruct(s, f32) for s in shapes],
        in_specs=[anywhere] * 8,
        out_specs=[anywhere] * 5,
        scratch_shapes=scratch,
        compiler_params=pltpu.CompilerParams(
            collective_id=0, has_side_effects=True, vmem_limit_bytes=56 << 20
        ),
        name="sage",
    )(*args)
    final = [(ROWS, HID), (ROWS, IN), (IN, HID), (IN, HID), (1, HID)]
    results = pl.pallas_call(
        write_out,
        out_shape=[jax.ShapeDtypeStruct(s, f32) for s in final],
        in_specs=[vmem] * 5,
        out_specs=[vmem] * 5,
        name="write_out",
    )(*[r.reshape(s) for r, s in zip(results, final)])
    return (*results[:4], results[4].reshape(HID))


def solution(mesh):
    rows = P(("group", "member"), None)
    return jax.shard_map(
        on_device,
        mesh=mesh,
        in_specs=(rows, P(), P(), P(), rows, rows, rows, P(("group", "member"))),
        out_specs=(rows, rows, P(), P(), P()),
        check_vma=False,
    )
```

time: 84.3 us -> 76 us (0.902)
  Pallas kernels: 82.9 us -> 74.4 us
    pallas_call x1, Pallas kernels: 81 us -> 72.5 us  [on_device(): pl.pallas_call(kernel, out_shape=[jax.ShapeDtypeStruct(s, f32) for s in s...]
where the time goes in v3:
time: 76 us; the launch traced here: 75.7 us
  Pallas kernels  74.4 us (98%)
  between operations  1.29 us (2%)
    pallas_call x1, Pallas kernels, on_device(): pl.pallas_call(kernel, out_shape=[jax.ShapeDtypeStruct(s, f32) for s in s...  72.5 us
    pallas_call x1, Pallas kernels, on_device(): pl.pallas_call(write_out, out_shape=[jax.ShapeDtypeStruct(s, f32) for s i...  1.84 us

profile of v3, /device:TPU:1, one launch (start us, length us, event | category | flops | bytes accessed | tf_op | source)
XLA Modules:
  0.0 75.7 jit_solution(17845062284750165450)
XLA Ops:
  1.3 72.5 %sage.1 = (f32[128,256]{1,0:T(8,128)}, f32[128,128]{1,0:T(8,128)}, f32[8,16,256]{2,1,0:T(8,128)}, f32[8,16,256]{2,1,0:T(8,128)}, f32[1,256]{1,0:T(1,128)}) custom-call(f32[128,128]{1,0:T(8,128)} %feat_h.1, f32[128,256]{1,0:T(8,128)} %w_self_h.1, f32[128,256]{1,0:T(8,128)} %w_neigh_h.1, f32[1,256]{1,0:T(1,128)} %bitcast.8, f32[128,256]{1,0:T(8,128)} %cot_h.1, ...), custom_call_target="tpu_custom_call" | custom-call | tf_op jit(solution)/shard_map/sage/pallas_call | solution.py:460
  73.8 1.8 %write_out.1 = (f32[128,256]{1,0:T(8,128)}, f32[128,128]{1,0:T(8,128)}, f32[128,256]{1,0:T(8,128)}, f32[128,256]{1,0:T(8,128)}, f32[1,256]{1,0:T(1,128)}) custom-call(f32[128,256]{1,0:T(8,128)} %get-tuple-element.15.refs_0_, f32[128,128]{1,0:T(8,128)} %get-tuple-element.16.refs_1_, f32[128,256]{1,0:T(8,128)} %bitcast.6, f32[128,256]{1,0:T(8,128)} %bitcast.7, ...), custom_call_target="tpu_custom_call" | custom-call | tf_op jit(solution)/shard_map/write_out/pallas_call | solution.py:472

commit v4 on v3

--- a/solution.py
+++ b/solution.py
@@ -53,13 +53,13 @@
 
 def kernel(
     feat_h, w_self_h, w_neigh_h, bias_h, cot_h, src_h, dst_h, cnt_h,
-    hid_o, fg_o, gs_o, gn_o, gb_o,
-    feat, w_self, w_neigh, bias, cot, e_src, e_dst, e_cnt, hid, fg, gb,
+    hid, fg, gs, gn, gb,
+    feat, w_self, w_neigh, bias, cot, e_src, e_dst, e_cnt,
     va, vb, acc, tab, own,
     hubs, hub_rows, erx, fts, frx, sums, sumrx, mgs, mgrx,
     g1s, g1rx, p2s, p2rx, p3s, p3rx, p4s, p4rx,
     bs, brx, hgs, hgrx, h2s, h2rx,
-    ssem, rsem, esem, isem, osem,
+    ssem, rsem, esem, isem,
 ):
     g, m = lax.axis_index("group"), lax.axis_index("member")
     core, z = lax.rem(m, 2), m // 2
@@ -145,8 +145,6 @@
     with jax.named_scope("entry_wait"):
         pl.semaphore_wait(barrier, M - 1 + G - 1)
 
-    hubs[m] = feat[0:1, :]
-    to_members(hubs.at[m], hubs, 0)
     over_members(fts, frx, 2)
 
     def edge_wait(slot):
@@ -165,6 +163,9 @@
     @pl.loop(1, M // 2)
     def _(n):
         edge_send(m, nth_slot(n, False))
+
+    hubs[m] = feat[0:1, :]
+    to_members(hubs.at[m], hubs, 0)
 
     def hand_on(quarter):
         @pl.loop(0, 4)
@@ -179,7 +180,7 @@
             edge_wait(nth_slot(4 * quarter + k, True))
 
     with jax.named_scope("edges_first"):
-        @pl.loop(1, 4)
+        @pl.loop(1, 8)
         def _(k):
             slot = nth_slot(k, False)
             edge_wait(slot)
@@ -275,17 +276,22 @@
     arrive("feat_wait", frx, M - 1, 2)
     with jax.named_scope("table"):
         table(frx)
-    arrive("hub_wait", hubs, M - 1, 0)
-
-    @pl.loop(1, G)
-    def _(step):
-        copy_to(hubs, hub_rows.at[g], 3, lax.rem(g + step, G), m).start()
-
-    hub_rows[g] = hubs[...]
     with jax.named_scope("forward"):
+        def share_hubs():
+            arrive("hub_wait", hubs, M - 1, 0)
+
+            @pl.loop(1, G)
+            def _(step):
+                copy_to(hubs, hub_rows.at[g], 3, lax.rem(g + step, G), m).start()
+
+            hub_rows[g] = hubs[...]
+
         def edges_in_time(i):
-            pl.when(i < 3)(lambda: hand_on(i + 1))
-            others(i)
+            with jax.named_scope("near_edges"):
+                pl.when((i == 1) | (i == 2))(lambda: hand_on(i + 1))
+            with jax.named_scope("other_edges"):
+                others(i)
+            pl.when(i == 3)(share_hubs)
 
         total = aggregate(True, edges_in_time)
     with jax.named_scope("sums"):
@@ -343,10 +349,7 @@
             for p in range(8):
                 hgs[8 * h + p, 0:M, :] = part[M * p : M * p + M, :]
                 hgs[8 * h + p, M : M + 8, :] = grad_b
-        over_groups(hgs, hgrx, 7)
         hid[...] = pre_act * sig
-        hid_out = pltpu.make_async_copy(hid, hid_o, osem.at[0])
-        hid_out.start()
         fg[...] = dot(pre_grad, w_self[...], NT)
 
     scale = 1.0 / (float(G * M * ROWS) ** 0.5)
@@ -392,45 +395,36 @@
         p4rx[g] = p4s[...]
 
     reduce_groups()
+    over_groups(hgs, hgrx, 7)
     arrive("mean_wait", mgrx, M - 1, 5)
     with jax.named_scope("backward"):
         table(mgrx)
         def reductions(i):
-            pl.when(i == 1)(reduce_hubs)
-            pl.when(i == 3)(reduce_members)
+            pl.when(i == 2)(reduce_members)
+            pl.when(i == 2)(reduce_hubs)
 
         total = aggregate(False, reductions)
     with jax.named_scope("tail"):
         unpack(bs, total)
         over_members(bs, brx, 12)
+        collect_members()
         arrive("hubsum_wait", h2rx, M - 1, 9)
         total = summed(h2rx, M)
         gb[:, 0:128] = total[1:2, :] * scale
         gb[:, 128:256] = total[2:3, :] * scale
         first = lax.broadcasted_iota(i32, (8, 128), 0) == 0
         fg[0:8, :] += jnp.where(first, jnp.broadcast_to(total[0:1, :], (8, 128)), 0.0)
-        collect_members()
         arrive("grad_wait", brx, M - 1, 12)
         fg[...] += joined(brx).T
-        late = [
-            pltpu.make_async_copy(fg, fg_o, osem.at[1]),
-            pltpu.make_async_copy(gb, gb_o, osem.at[2]),
-            pltpu.make_async_copy(p4rx.at[pl.ds(0, G // 2)], gs_o, osem.at[3]),
-            pltpu.make_async_copy(p4rx.at[pl.ds(G // 2, G // 2)], gn_o, osem.at[4]),
-        ]
-        for copy in late[0:2]:
-            copy.start()
         arrive("p4_wait", p4rx, G - 1, 11)
-        for copy in late[2:4]:
-            copy.start()
+        gs[...] = p4rx[0 : G // 2]
+        gn[...] = p4rx[G // 2 : G]
 
     for buf, n, k in (
         (hubs, M, 0), (erx, M, 1), (frx, M, 2), (hub_rows, G, 3), (sumrx, M, 4), (mgrx, M, 5), (g1rx, G, 6),
         (hgrx, G, 7), (p2rx, M, 8), (h2rx, M, 9), (p3rx, M, 10), (p4rx, G, 11), (brx, M, 12),
     ):
         wait(buf, n - 1, ssem.at[k])
-    for copy in [hid_out] + late:
-        copy.wait()
 
 
 def write_out(*refs):
@@ -444,7 +438,6 @@
     lines = pltpu.VMEM((M, 1, 128), f32)
     args = [features, w_self, w_neigh, bias.reshape(1, HID), cotangent, edge_src, edge_dst, edge_count.reshape(1, 1)]
     scratch = [pltpu.VMEM(a.shape, a.dtype) for a in args] + [
-        pltpu.VMEM((ROWS, HID), f32), pltpu.VMEM((ROWS, IN), f32), pltpu.VMEM((1, HID), f32),
         pltpu.VMEM((4 * N, 8 * HI_V + 16, 256), bf16), pltpu.VMEM((4 * N, 8 * HI_V + 16, 256), bf16),
         pltpu.VMEM((LO, 8 * HI_V + 16), f32), pltpu.VMEM((8 * HI_V, LO), bf16),
         pltpu.VMEM((LO, HI_H * ROWS), f32),
@@ -454,14 +447,14 @@
         pltpu.VMEM((1, 128), f32), lines, pltpu.VMEM((16, HID), f32), pltpu.VMEM((G, 16, HID), f32),
         quads, quads, pltpu.VMEM((G, M + 8, 128), f32), pltpu.VMEM((G, M + 8, 128), f32), quads, quads,
         pltpu.SemaphoreType.DMA((13,)), pltpu.SemaphoreType.DMA((13,)), pltpu.SemaphoreType.DMA((M,)),
-        pltpu.SemaphoreType.DMA((8,)), pltpu.SemaphoreType.DMA((5,)),
+        pltpu.SemaphoreType.DMA((8,)),
     ]
     shapes = [(ROWS, HID), (ROWS, IN), (G // 2, 16, HID), (G // 2, 16, HID), (1, HID)]
     results = pl.pallas_call(
         kernel,
-        out_shape=[jax.ShapeDtypeStruct(s, f32) for s in shapes],
+        out_shape=[pltpu.VMEM(s, f32) for s in shapes],
         in_specs=[anywhere] * 8,
-        out_specs=[anywhere] * 5,
+        out_specs=[vmem] * 5,
         scratch_shapes=scratch,
         compiler_params=pltpu.CompilerParams(
             collective_id=0, has_side_effects=True, vmem_limit_bytes=56 << 20
@@ -474,6 +467,7 @@
         out_shape=[jax.ShapeDtypeStruct(s, f32) for s in final],
         in_specs=[vmem] * 5,
         out_specs=[vmem] * 5,
+        compiler_params=pltpu.CompilerParams(vmem_limit_bytes=4 << 20),
         name="write_out",
     )(*[r.reshape(s) for r, s in zip(results, final)])
     return (*results[:4], results[4].reshape(HID))

time: 76 us -> 74 us (0.974)
  Pallas kernels: 74.4 us -> 72.6 us
    pallas_call x1, Pallas kernels: 1.84 us -> 0.8 us  [on_device(): pl.pallas_call(write_out, out_shape=[jax.ShapeDtypeStruct(s, f32) for s i...]
where the time goes in v4:
time: 74 us; the launch traced here: 73.9 us
  Pallas kernels  72.6 us (98%)
  between operations  1.29 us (2%)
    pallas_call x1, Pallas kernels, on_device(): pl.pallas_call(kernel, out_shape=[pltpu.VMEM(s, f32) for s in shapes], in...  71.8 us

profile of v4, /device:TPU:1, one launch (start us, length us, event | category | flops | bytes accessed | tf_op | source)
XLA Modules:
  0.0 73.9 jit_solution(3696427373769585322)
XLA Ops:
  1.3 71.8 %sage.1 = (f32[128,256]{1,0:T(8,128)S(1)}, f32[128,128]{1,0:T(8,128)S(1)}, f32[8,16,256]{2,1,0:T(8,128)S(1)}, f32[8,16,256]{2,1,0:T(8,128)S(1)}, f32[1,256]{1,0:T(1,128)S(1)}) custom-call(f32[128,128]{1,0:T(8,128)} %feat_h.1, f32[128,256]{1,0:T(8,128)} %w_self_h.1, f32[128,256]{1,0:T(8,128)} %w_neigh_h.1, f32[1,256]{1,0:T(1,128)} %bitcast.8, ...), custom_call_target="tpu_custom_call" | custom-call | tf_op jit(solution)/shard_map/sage/pallas_call | solution.py:453
  73.1 0.8 %write_out.1 = (f32[128,256]{1,0:T(8,128)}, f32[128,128]{1,0:T(8,128)}, f32[128,256]{1,0:T(8,128)}, f32[128,256]{1,0:T(8,128)}, f32[1,256]{1,0:T(1,128)}) custom-call(f32[128,256]{1,0:T(8,128)S(1)} %get-tuple-element.15.refs_0_, f32[128,128]{1,0:T(8,128)S(1)} %get-tuple-element.16.refs_1_, f32[128,256]{1,0:T(8,128)S(1)} %bitcast.6, f32[128,256]{1,0:T(8,128)S(1)} %bitcast.7, ...), custom_call_target="tpu_custom_call" | custom-call | tf_op jit(solution)/shard_map/write_out/pallas_call | solution.py:465

commit v5 on v4

--- a/solution.py
+++ b/solution.py
@@ -414,17 +414,16 @@
         gb[:, 128:256] = total[2:3, :] * scale
         first = lax.broadcasted_iota(i32, (8, 128), 0) == 0
         fg[0:8, :] += jnp.where(first, jnp.broadcast_to(total[0:1, :], (8, 128)), 0.0)
+        for buf, n, k in (
+            (hubs, M, 0), (erx, M, 1), (frx, M, 2), (hub_rows, G, 3), (sumrx, M, 4), (mgrx, M, 5), (g1rx, G, 6),
+            (hgrx, G, 7), (p2rx, M, 8), (h2rx, M, 9), (p3rx, M, 10), (p4rx, G, 11), (brx, M, 12),
+        ):
+            wait(buf, n - 1, ssem.at[k])
         arrive("grad_wait", brx, M - 1, 12)
         fg[...] += joined(brx).T
         arrive("p4_wait", p4rx, G - 1, 11)
         gs[...] = p4rx[0 : G // 2]
         gn[...] = p4rx[G // 2 : G]
-
-    for buf, n, k in (
-        (hubs, M, 0), (erx, M, 1), (frx, M, 2), (hub_rows, G, 3), (sumrx, M, 4), (mgrx, M, 5), (g1rx, G, 6),
-        (hgrx, G, 7), (p2rx, M, 8), (h2rx, M, 9), (p3rx, M, 10), (p4rx, G, 11), (brx, M, 12),
-    ):
-        wait(buf, n - 1, ssem.at[k])
 
 
 def write_out(*refs):

time: 74 us -> 74 us (level)
  no operation moved by 1% of the time
where the time goes in v5:
time: 74 us; the launch traced here: 73.9 us
  Pallas kernels  72.6 us (98%)
  between operations  1.29 us (2%)
    pallas_call x1, Pallas kernels, on_device(): pl.pallas_call(kernel, out_shape=[pltpu.VMEM(s, f32) for s in shapes], in...  71.8 us

profile of v5, /device:TPU:1, one launch (start us, length us, event | category | flops | bytes accessed | tf_op | source)
XLA Modules:
  0.0 73.9 jit_solution(10417608908894529785)
XLA Ops:
  1.3 71.8 %sage.1 = (f32[128,256]{1,0:T(8,128)S(1)}, f32[128,128]{1,0:T(8,128)S(1)}, f32[8,16,256]{2,1,0:T(8,128)S(1)}, f32[8,16,256]{2,1,0:T(8,128)S(1)}, f32[1,256]{1,0:T(1,128)S(1)}) custom-call(f32[128,128]{1,0:T(8,128)} %feat_h.1, f32[128,256]{1,0:T(8,128)} %w_self_h.1, f32[128,256]{1,0:T(8,128)} %w_neigh_h.1, f32[1,256]{1,0:T(1,128)} %bitcast.8, ...), custom_call_target="tpu_custom_call" | custom-call | tf_op jit(solution)/shard_map/sage/pallas_call | solution.py:452
  73.1 0.8 %write_out.1 = (f32[128,256]{1,0:T(8,128)}, f32[128,128]{1,0:T(8,128)}, f32[128,256]{1,0:T(8,128)}, f32[128,256]{1,0:T(8,128)}, f32[1,256]{1,0:T(1,128)}) custom-call(f32[128,256]{1,0:T(8,128)S(1)} %get-tuple-element.15.refs_0_, f32[128,128]{1,0:T(8,128)S(1)} %get-tuple-element.16.refs_1_, f32[128,256]{1,0:T(8,128)S(1)} %bitcast.6, f32[128,256]{1,0:T(8,128)S(1)} %bitcast.7, ...), custom_call_target="tpu_custom_call" | custom-call | tf_op jit(solution)/shard_map/write_out/pallas_call | solution.py:464
